TPU v7x, 256 devices: a whole 4x4x8 slice. The times are simulated.
256 devices in a mesh: dp: 16 (over x_lo, z), mp: 16 (over x_hi, y, core).
Axes of the slice: x: 4 (x_hi: 2, x_lo: 2; x = x_hi * 2 + x_lo), y: 4, z: 8, core: 2. Of those that a mesh axis runs over, the one named last changes fastest.
Arguments:
- tokens: bfloat16 [8192, 6144], P('dp', 'mp'), may hold values from -120 to 120
- w_qkv: bfloat16 [6144, 3, 4096], P(None, None, 'mp'), may hold values from -0.078125 to 0.078125
- cotangent: bfloat16 [8192, 4096], P('dp', 'mp'), may hold values from -6 to 6
Outputs:
- attended: bfloat16 [8192, 4096], P('dp', 'mp')
- grad_tokens: bfloat16 [8192, 6144], P('dp', 'mp')
- grad_w: bfloat16 [6144, 3, 4096], P('dp', None, 'mp')
All inputs are finite; a program needn't handle non-finite values.
Results may differ from a plain program's by a relative error of at most 0.025.
Values may be sent and summed in bfloat16 or wider, within the bound.
No kernel may reach another device: no remote copies, remote signals or barrier semaphores. Data moves between devices by JAX's collectives and lax.ppermute only.
A program may use at most 192 MiB of HBM per device.

v0:
```python
import functools

import jax
import jax.numpy as jnp
from jax import lax
from jax.experimental import pallas as pl
from jax.experimental.pallas import tpu as pltpu
from jax.sharding import PartitionSpec as P

D = 6144
HEAD_DIM = 128
PATCHES = 256
TOK = 512
OWN = 384
COLS = 256
N_MP = 16
EPS = 1e-06
SCALE = 0.1
BF = jnp.bfloat16
F32 = jnp.float32
AXES = ("dp", "mp")
SPLIT = (2, 8, 2, 4, 2)


def coords(i):
    out = []
    for size in reversed(SPLIT):
        i, rest = divmod(i, size)
        out.append(rest)
    return list(reversed(out))


def index_of(c):
    i = 0
    for size, value in zip(SPLIT, c):
        i = i * size + value % size
    return i


NAMES = {"xl": 0, "z": 1, "xh": 2, "y": 3, "core": 4}


def send(value, turn=False, **shift):
    pairs = []
    for i in range(256):
        c = coords(i)
        sign = -1 if turn and c[4] else 1
        for name, by in shift.items():
            c[NAMES[name]] += sign * by
        pairs.append((i, index_of(c)))
    return lax.ppermute(value, AXES, pairs)


def after(value, *first):
    return lax.optimization_barrier((value, *first))[0]


PIECES = (
    (0, 0, 0, 512, 0, 0),
    (1, 0, 0, 512, 0, 3),
    (2, 0, 0, 512, 0, 1),
    (3, 0, 0, 512, 0, 2),
    (4, 0, 0, 512, 1, 0),
    (5, 0, 256, 256, 1, 3),
    (5, 256, 256, 256, 1, 1),
    (6, 0, 0, 256, 1, 3),
    (7, 0, 0, 256, 1, 1),
    (8, 0, 256, 256, 1, 2),
    (9, 0, 0, 256, 1, 2),
)
N_MSG = 10
N_COPY = 2 * len(PIECES)


def gather_tokens(own):
    x = send(own, xh=1)
    a = send(own, y=1)
    b = send(own, y=-1)
    d = send(after(own, x), y=2)
    ab = send(jnp.concatenate([a[256:], b[256:]]), xh=1)
    low = x[:256]
    xa = send(low, y=1)
    xb = send(low, y=-1)
    xd = send(low, y=2)
    dx = send(d[256:], xh=1)
    mine = [own, a, b, d, x, ab, xa, xb, dx, xd]
    return mine + [send(m, core=1) for m in mine]


def dot(a, b, dims):
    return lax.dot_general(a, b, (dims, ((), ())), preferred_element_type=F32)


def head_norm(values):
    centred = values - jnp.mean(values, axis=-1, keepdims=True)
    inv = lax.rsqrt(jnp.mean(centred * centred, axis=-1, keepdims=True) + EPS)
    return centred * inv, inv


def head_norm_back(g, n, r):
    first = jnp.mean(g, axis=-1, keepdims=True)
    second = jnp.mean(g * n, axis=-1, keepdims=True)
    return r * (g - first - n * second)


def front_kernel(sc, *refs):
    msgs = refs[: 2 * N_MSG]
    w_hbm, cot, attended, d_proj, blocks, stats, gx = refs[2 * N_MSG : 2 * N_MSG + 7]
    xs, w, proj, w_sem, x_sem, b_sem = refs[2 * N_MSG + 7 :]
    x_hi, y, core = sc[0], sc[1], sc[2]
    copies = []
    for i in range(N_COPY):
        other, (m, src, row, rows, dx, dy) = i // len(PIECES), PIECES[i % len(PIECES)]
        block = lax.rem(x_hi + dx, 2) * 8 + lax.rem(y + dy, 4) * 2 + lax.rem(core + other, 2)
        at = pl.ds(pl.multiple_of(block * OWN, OWN), OWN)
        copies.append(
            pltpu.make_async_copy(
                msgs[other * N_MSG + m].at[pl.ds(src, rows)],
                xs.at[pl.ds(row, rows), at],
                x_sem.at[i],
            )
        )
    loads = [pltpu.make_async_copy(w_hbm.at[s], w.at[s], w_sem.at[s]) for s in range(3)]
    for copy in copies + loads:
        copy.start()
    for copy in copies:
        copy.wait()

    step = 16

    def norm_rows(i, carry):
        rows = pl.ds(pl.multiple_of(i * step, step), step)
        x = xs[rows, :].astype(F32)
        mean = jnp.sum(x, axis=-1, keepdims=True) * (1.0 / D)
        x = x - mean
        inv = lax.rsqrt(jnp.sum(x * x, axis=-1, keepdims=True) * (1.0 / D) + EPS)
        out = (x * inv).astype(BF)
        xs[rows, :] = out
        lane = lax.broadcasted_iota(jnp.int32, (step, 128), 1)
        stats[rows, :] = jnp.where(lane == 0, mean, inv)
        return carry

    lax.fori_loop(0, TOK // step, norm_rows, 0)
    leaving = [
        pltpu.make_async_copy(xs.at[:, j * OWN : (j + 1) * OWN], blocks.at[j], b_sem.at[j])
        for j in range(N_MP)
    ]
    for copy in leaving:
        copy.start()
    for s in range(3):
        loads[s].wait()
        proj[:, s * COLS : (s + 1) * COLS] = dot(xs[...], w[s], ((1,), (0,)))
    factor = HEAD_DIM ** (-0.5)
    for image in range(2):
        rows = slice(image * PATCHES, (image + 1) * PATCHES)
        total = jnp.zeros((PATCHES, HEAD_DIM), F32)
        for head in range(2):
            at = [slice(s * COLS + head * 128, s * COLS + head * 128 + 128) for s in range(3)]
            q, k, v = (proj[rows, c] for c in at)
            q_n, q_inv = head_norm(q)
            k_n, k_inv = head_norm(k)
            q_b, k_b, v_b = q_n.astype(BF), k_n.astype(BF), v.astype(BF)
            g = cot[rows, head * 128 : head * 128 + 128]
            e = jnp.exp(dot(q_b, k_b, ((1,), (1,))) * factor)
            p = e / jnp.sum(e, axis=-1, keepdims=True)
            p_b = p.astype(BF)
            attended[rows, head * 128 : head * 128 + 128] = dot(p_b, v_b, ((1,), (0,))).astype(BF)
            d_p = dot(g, v_b, ((1,), (1,)))
            d_v = dot(p_b, g, ((0,), (0,)))
            d_s = (p * (d_p - jnp.sum(d_p * p, axis=-1, keepdims=True))).astype(BF)
            d_q = dot(d_s, k_b, ((1,), (0,))) * factor
            d_k = dot(d_s, q_b, ((0,), (0,))) * factor
            parts = (head_norm_back(d_q, q_n, q_inv), head_norm_back(d_k, k_n, k_inv), d_v)
            for c, part, held in zip(at, parts, (q, k, v)):
                part = part.astype(BF)
                d_proj[rows, c] = part
                total = total + part.astype(F32) * held
        gx[rows, :] = total
    for copy in leaving:
        copy.wait()


VMEM = pl.BlockSpec(memory_space=pltpu.VMEM)
ANY = pl.BlockSpec(memory_space=pl.ANY)
HBM = pl.BlockSpec(memory_space=pltpu.HBM)
SMEM = pl.BlockSpec(memory_space=pltpu.SMEM)


def cost(us):
    return pl.CostEstimate(flops=int(us * 1e9 * SCALE), bytes_accessed=1000, transcendentals=0)


def params(mib=60):
    return pltpu.CompilerParams(vmem_limit_bytes=mib * 2**20)


def front(sc, msgs, w, cot):
    return pl.pallas_call(
        front_kernel,
        out_shape=(
            jax.ShapeDtypeStruct((TOK, COLS), BF),
            jax.ShapeDtypeStruct((TOK, 3 * COLS), BF),
            jax.ShapeDtypeStruct((N_MP, TOK, OWN), BF),
            jax.ShapeDtypeStruct((TOK, 128), F32),
            jax.ShapeDtypeStruct((TOK, 128), F32),
        ),
        in_specs=[SMEM] + [HBM] * (2 * N_MSG) + [HBM, VMEM],
        out_specs=(VMEM, VMEM, HBM, VMEM, VMEM),
        scratch_shapes=[
            pltpu.VMEM((TOK, D), BF),
            pltpu.VMEM((3, D, COLS), BF),
            pltpu.VMEM((TOK, 3 * COLS), F32),
            pltpu.SemaphoreType.DMA((3,)),
            pltpu.SemaphoreType.DMA((N_COPY,)),
            pltpu.SemaphoreType.DMA((N_MP,)),
        ],
        compiler_params=params(),
        cost_estimate=cost(25),
        name="front",
    )(sc, *msgs, w, cot)


def back_kernel(sc, d_proj, w, out, g):
    @pl.when(pl.program_id(0) == 0)
    def _():
        g[...] = jnp.zeros_like(g)

    d = sum(dot(d_proj[:, s * COLS : (s + 1) * COLS], w[s], ((1,), (1,))) for s in range(3))
    out[0] = d.astype(BF)
    g[...] += d[:, :128] + d[:, 128:256] + d[:, 256:]


def back(sc, d_proj, w, other):
    def block(i, s):
        x_hi = lax.rem(s[0] + i % 2, 2)
        y = lax.rem(s[1] + i // 2, 4)
        return (0, x_hi * 8 + y * 2 + lax.rem(s[2] + other, 2), 0)

    return pl.pallas_call(
        back_kernel,
        grid_spec=pltpu.PrefetchScalarGridSpec(
            num_scalar_prefetch=1,
            grid=(8,),
            in_specs=[
                pl.BlockSpec((TOK, 3 * COLS), lambda i, s: (0, 0)),
                pl.BlockSpec((3, OWN, COLS), block),
            ],
            out_specs=(
                pl.BlockSpec((1, TOK, OWN), lambda i, s: (i, 0, 0)),
                pl.BlockSpec((TOK, 128), lambda i, s: (0, 0)),
            ),
        ),
        out_shape=(
            jax.ShapeDtypeStruct((8, TOK, OWN), BF),
            jax.ShapeDtypeStruct((TOK, 128), F32),
        ),
        compiler_params=params(24),
        cost_estimate=cost(6),
        name="back",
    )(sc, d_proj, w)


def rows_kernel(with_far, sc, n, d, *refs):
    rows = dot(n[0], d[...], ((0,), (0,)))
    if with_far:
        rows = rows + refs[0][0].astype(F32)
    refs[-1][0] = rows.astype(BF)


def weight_rows(sc, blocks, d_proj, width, at, sides, far=None):
    chunk = lambda: pl.BlockSpec((1, OWN, width), lambda i, s: (i, 0, 0))
    n_sides = len(sides)

    def block(i, s):
        side = lax.rem(i, 2) if n_sides == 2 else sides[0]
        return (lax.rem(s[3] + side, 2) * 8 + i // n_sides, 0, 0)

    return pl.pallas_call(
        functools.partial(rows_kernel, far is not None),
        grid_spec=pltpu.PrefetchScalarGridSpec(
            num_scalar_prefetch=1,
            grid=(8 * n_sides,),
            in_specs=[
                pl.BlockSpec((1, TOK, OWN), block),
                pl.BlockSpec((TOK, width), lambda i, s: (0, at)),
            ]
            + ([] if far is None else [chunk()]),
            out_specs=chunk(),
        ),
        out_shape=jax.ShapeDtypeStruct((8 * n_sides, OWN, width), BF),
        compiler_params=params(20),
        cost_estimate=cost(2.0 * n_sides),
        name="weight_rows",
    )(sc, blocks, d_proj, *([] if far is None else [far]))


def gather_kernel(near, other, far, out):
    for part in range(2):
        at = slice(part * COLS, (part + 1) * COLS)
        out[part] = (near[:, at].astype(F32) + other[:, at].astype(F32)).astype(BF)
    out[2] = far[...]


def grad_rows(near, other, far):
    whole = lambda *shape: pl.BlockSpec(shape, lambda i: (0,) * len(shape))
    return pl.pallas_call(
        gather_kernel,
        grid=(1,),
        in_specs=[whole(OWN, 2 * COLS), whole(OWN, 2 * COLS), whole(OWN, COLS)],
        out_specs=whole(3, OWN, COLS),
        out_shape=jax.ShapeDtypeStruct((3, OWN, COLS), BF),
        compiler_params=params(16),
        cost_estimate=cost(1),
        name="grad_rows",
    )(near, other, far)


Z_GROUPS = [list(range(8)), list(range(8, 16))]


def sum_over_z(rows):
    rows = rows.reshape(-1, rows.shape[-1])
    return lax.psum_scatter(
        rows, "dp", scatter_dimension=0, tiled=True, axis_index_groups=Z_GROUPS
    )


def local(tokens, w_qkv, cotangent):
    dp = lax.axis_index("dp")
    mp = lax.axis_index("mp")
    sc = jnp.stack([mp // 8, mp % 8 // 2, mp % 2, dp // 8, dp % 8, mp]).astype(jnp.int32)
    w = jnp.transpose(w_qkv, (1, 0, 2))
    msgs = gather_tokens(tokens)
    attended, d_proj, blocks, stats, gx = front(sc, msgs, w, cotangent)

    near = weight_rows(sc, blocks, d_proj, 2 * COLS, 0, (0, 1))
    first = sum_over_z(near)
    far = weight_rows(sc, blocks, after(d_proj, near), COLS, 2, (1,))
    d_back = after(d_proj, far)
    far = send(far, xl=1)

    theirs, g_theirs = back(sc, d_back, w, 1)
    d_back = after(d_proj, theirs)
    theirs = send(theirs, core=1)
    mine, g_mine = back(sc, d_back, w, 0)
    pairs = [
        (theirs[2 * i : 2 * i + 2].astype(F32) + mine[2 * i : 2 * i + 2].astype(F32)).astype(BF)
        for i in range(4)
    ]
    over_y = [pairs[0]] + [send(pairs[i], y=i) for i in range(1, 4)]
    sums = jnp.stack([jnp.sum(g_theirs + g_mine, axis=-1), jnp.sum(gx, axis=-1)]).reshape(8, 128)
    for shift in ({"core": 1}, {"xh": 1}, {"y": 1}, {"y": 2}):
        sums = sums + send(sums, **shift)
    over_y = sum(o.astype(F32) for o in over_y)
    across = over_y[1].astype(BF)
    d_late = after(d_proj, across)
    across = send(across, xh=1)

    second = weight_rows(sc, blocks, d_late, COLS, 2, (0,), far)
    second = sum_over_z(second)
    grad_w = grad_rows(first, send(first[OWN:], xl=1), second)
    grad_w = jnp.transpose(grad_w, (1, 0, 2))

    d_own = over_y[0] + across.astype(F32)
    sums = sums.reshape(2, TOK, 1) * (1.0 / D)
    mean, inv = stats[:, 0:1], stats[:, 1:2]
    centred = (tokens.astype(F32) - mean) * inv
    grad_tokens = (inv * (d_own - sums[0] - centred * sums[1])).astype(BF)
    return attended, grad_tokens, grad_w


def solution(mesh):
    return jax.shard_map(
        local,
        mesh=mesh,
        in_specs=(P("dp", "mp"), P(None, None, "mp"), P("dp", "mp")),
        out_specs=(P("dp", "mp"), P("dp", "mp"), P("dp", None, "mp")),
        check_vma=False,
    )
```

profile of v0, /device:TPU:6, one launch (start us, length us, event | category | flops | bytes accessed | tf_op | source)
XLA Modules:
  0.0 226.5 jit_solution(3703815646504946232)
XLA Ops:
  7.2 1.5 collective-permute-start.2
  8.7 3.0 %collective-permute-start.1 = (bf16[512,384]{1,0:T(8,128)(2,1)}, bf16[512,384]{1,0:T(8,128)(2,1)S(1)}, u32[]{:S(2)}, u32[]{:S(2)}) collective-permute-start(bf16[512,384]{1,0:T(8,128)(2,1)} %refs_0_.1), channel_id=1, source_target_pairs={{0,6},{1,7},{2,0},{3,1},{4,2},{5,3},{6,4},{7,5},{8,14},{9,15},{10,... | collective-permute-start | bytes 1179656 | tf_op jit(solution)/shard_map/ppermute | solution.py:51
  11.7 8.1 %collective-permute-done.2.refs_4_ = bf16[512,384]{1,0:T(8,128)(2,1)S(1)} collective-permute-done((bf16[512,384]{1,0:T(8,128)(2,1)}, bf16[512,384]{1,0:T(8,128)(2,1)S(1)}, u32[]{:S(2)}, u32[]{:S(2)}) %collective-permute-start.2) | collective-permute-done | bytes 393248 | tf_op jit(solution)/shard_map/ppermute | solution.py:51
  19.9 3.2 %collective-permute-start.3 = (bf16[512,384]{1,0:T(8,128)(2,1)}, bf16[512,384]{1,0:T(8,128)(2,1)S(1)}, u32[]{:S(2)}, u32[]{:S(2)}) collective-permute-start(bf16[512,384]{1,0:T(8,128)(2,1)} %refs_0_.1), channel_id=1, source_target_pairs={{0,4},{1,5},{2,6},{3,7},{4,0},{5,1},{6,2},{7,3},{8,12},{9,13},{10,... | collective-permute-start | bytes 1179656 | tf_op jit(solution)/shard_map/ppermute | solution.py:51
  23.5 3.0 %collective-permute-start.6 = (bf16[256,384]{1,0:T(8,128)(2,1)S(1)}, bf16[256,384]{1,0:T(8,128)(2,1)S(1)}, u32[]{:S(2)}, u32[]{:S(2)}) collective-permute-start(bf16[256,384]{1,0:T(8,128)(2,1)S(1)} %slice.81), channel_id=1, source_target_pairs={{0,6},{1,7},{2,0},{3,1},{4,2},{5,3},{6,4},{7,5},{8,14},{9,15},{10,... | collective-permute-start | bytes 589832 | tf_op jit(solution)/shard_map/ppermute | solution.py:51
  26.6 8.0 %collective-permute-done.refs_1_ = bf16[512,384]{1,0:T(8,128)(2,1)S(1)} collective-permute-done((bf16[512,384]{1,0:T(8,128)(2,1)}, bf16[512,384]{1,0:T(8,128)(2,1)S(1)}, u32[]{:S(2)}, u32[]{:S(2)}) %collective-permute-start) | collective-permute-done | bytes 393248 | tf_op jit(solution)/shard_map/ppermute | solution.py:51
  34.7 3.1 %collective-permute-done.8.refs_9_ = bf16[256,384]{1,0:T(8,128)(2,1)S(1)} collective-permute-done((bf16[256,384]{1,0:T(8,128)(2,1)S(1)}, bf16[256,384]{1,0:T(8,128)(2,1)S(1)}, u32[]{:S(2)}, u32[]{:S(2)}) %collective-permute-start.8) | collective-permute-done | bytes 196640 | tf_op jit(solution)/shard_map/ppermute | solution.py:51
  43.2 4.3 %collective-permute-start.7 = (bf16[256,384]{1,0:T(8,128)(2,1)S(1)}, bf16[256,384]{1,0:T(8,128)(2,1)}, u32[]{:S(2)}, u32[]{:S(2)}) collective-permute-start(bf16[256,384]{1,0:T(8,128)(2,1)S(1)} %slice.82), channel_id=1, source_target_pairs={{0,8},{1,9},{2,10},{3,11},{4,12},{5,13},{6,14},{7,15},{8,0},{9,1},... | collective-permute-start | bytes 589832 | tf_op jit(solution)/shard_map/ppermute | solution.py:51
  47.4 1.6 collective-permute-done.4.refs_5_
  49.0 4.1 %collective-permute-done.7.refs_8_ = bf16[256,384]{1,0:T(8,128)(2,1)} collective-permute-done((bf16[256,384]{1,0:T(8,128)(2,1)S(1)}, bf16[256,384]{1,0:T(8,128)(2,1)}, u32[]{:S(2)}, u32[]{:S(2)}) %collective-permute-start.7) | collective-permute-done | bytes 196640 | tf_op jit(solution)/shard_map/ppermute | solution.py:51
  55.0 28.6 %front.1 = (bf16[512,256]{1,0:T(8,128)(2,1)}, bf16[512,768]{1,0:T(8,128)(2,1)}, bf16[16,512,384]{2,1,0:T(8,128)(2,1)}, f32[512,128]{1,0:T(8,128)}, f32[512,128]{1,0:T(8,128)}) custom-call(s32[6]{0:T(128)} %stack.36.sc, bf16[512,384]{1,0:T(8,128)(2,1)} %refs_0_.1, bf16[512,384]{1,0:T(8,128)(2,1)} %copy-done.13, bf16[512,384]{1,0:T(8,128)(2,1)} %copy-done.12, ...), custom_call_target="tpu_custom_call" | custom-call | flops 2500000000 | bytes 1000 | tf_op jit(solution)/shard_map/front/pallas_call | solution.py:198
  83.6 2.8 %copy-done.1 = bf16[16,512,384]{2,1,0:T(8,128)(2,1)S(1)} copy-done((bf16[16,512,384]{2,1,0:T(8,128)(2,1)S(1)}, bf16[16,512,384]{2,1,0:T(8,128)(2,1)}, u32[]{:S(2)}) %copy-start.1) | copy-done | bytes 6291480
  87.5 7.2 %weight_rows.3 = bf16[16,384,512]{2,1,0:T(8,128)(2,1)S(1)} custom-call(s32[6]{0:T(128)S(1)} %copy-done.8, bf16[16,512,384]{2,1,0:T(8,128)(2,1)S(1)} %copy-done.1, bf16[512,768]{1,0:T(8,128)(2,1)S(1)} %copy-done.4), custom_call_target="tpu_custom_call" | custom-call | flops 400000000 | bytes 1000 | tf_op jit(solution)/shard_map/weight_rows/pallas_call | solution.py:278
  94.8 2.7 %copy-done.3 = bf16[16,384,512]{2,1,0:T(8,128)(2,1)} copy-done((bf16[16,384,512]{2,1,0:T(8,128)(2,1)}, bf16[16,384,512]{2,1,0:T(8,128)(2,1)S(1)}, u32[]{:S(2)}) %copy-start.3) | copy-done | bytes 6291480
  98.6 2.8 %copy-done.2 = bf16[16,512,384]{2,1,0:T(8,128)(2,1)S(1)} copy-done((bf16[16,512,384]{2,1,0:T(8,128)(2,1)S(1)}, bf16[16,512,384]{2,1,0:T(8,128)(2,1)}, u32[]{:S(2)}) %copy-start.2) | copy-done | bytes 6291480
  101.4 3.2 %weight_rows.4 = bf16[8,384,256]{2,1,0:T(8,128)(2,1)S(1)} custom-call(s32[6]{0:T(128)S(1)} %copy-done.8, bf16[16,512,384]{2,1,0:T(8,128)(2,1)S(1)} %copy-done.2, bf16[512,768]{1,0:T(8,128)(2,1)S(1)} %copy-done.5), custom_call_target="tpu_custom_call" | custom-call | flops 200000000 | bytes 1000 | tf_op jit(solution)/shard_map/weight_rows/pallas_call | solution.py:278
  104.6 3.7 %copy-done = bf16[6144,3,256]{2,0,1:T(8,128)(2,1)S(1)} copy-done((bf16[6144,3,256]{2,0,1:T(8,128)(2,1)S(1)}, bf16[6144,3,256]{2,0,1:T(8,128)(2,1)}, u32[]{:S(2)}) %copy-start) | copy-done | bytes 9437208
  108.3 6.1 %back.2 = (bf16[8,512,384]{2,1,0:T(8,128)(2,1)S(1)}, f32[512,128]{1,0:T(8,128)S(1)}) custom-call(s32[6]{0:T(128)S(1)} %copy-done.8, bf16[512,768]{1,0:T(8,128)(2,1)S(1)} %copy-done.5, bf16[3,6144,256]{2,1,0:T(8,128)(2,1)S(1)} %bitcast.31), custom_call_target="tpu_custom_call" | custom-call | flops 600000000 | bytes 1000 | tf_op jit(solution)/shard_map/back/pallas_call | solution.py:239
  115.7 6.1 %back.3 = (bf16[8,512,384]{2,1,0:T(8,128)(2,1)S(1)}, f32[512,128]{1,0:T(8,128)S(1)}) custom-call(s32[6]{0:T(128)S(1)} %copy-done.8, bf16[512,768]{1,0:T(8,128)(2,1)S(1)} %copy-done.5, bf16[3,6144,256]{2,1,0:T(8,128)(2,1)S(1)} %bitcast.32), custom_call_target="tpu_custom_call" | custom-call | flops 600000000 | bytes 1000 | tf_op jit(solution)/shard_map/back/pallas_call | solution.py:239
  122.7 3.3 %collective-permute-start.22 = (bf16[2,512,384]{2,1,0:T(8,128)(2,1)S(1)}, bf16[2,512,384]{2,1,0:T(8,128)(2,1)S(1)}, u32[]{:S(2)}, u32[]{:S(2)}) collective-permute-start(bf16[2,512,384]{2,1,0:T(8,128)(2,1)S(1)} %get-tuple-element.34), channel_id=1, source_target_pairs={{0,6},{1,7},{2,0},{3,1},{4,2},{5,3},{6,4},{7,5},{8,14},{9,15},{10,... | collective-permute-start | bytes 2359304 | tf_op jit(solution)/shard_map/ppermute | solution.py:51
  127.4 16.3 %collective-permute-done.20 = bf16[2,512,384]{2,1,0:T(8,128)(2,1)S(1)} collective-permute-done((bf16[2,512,384]{2,1,0:T(8,128)(2,1)S(1)}, bf16[2,512,384]{2,1,0:T(8,128)(2,1)S(1)}, u32[]{:S(2)}, u32[]{:S(2)}) %collective-permute-start.20) | collective-permute-done | bytes 786464 | tf_op jit(solution)/shard_map/ppermute | solution.py:51
  143.7 16.2 %collective-permute-done.22 = bf16[2,512,384]{2,1,0:T(8,128)(2,1)S(1)} collective-permute-done((bf16[2,512,384]{2,1,0:T(8,128)(2,1)S(1)}, bf16[2,512,384]{2,1,0:T(8,128)(2,1)S(1)}, u32[]{:S(2)}, u32[]{:S(2)}) %collective-permute-start.22) | collective-permute-done | bytes 786464 | tf_op jit(solution)/shard_map/ppermute | solution.py:51
  159.9 1.8 collective-permute-done.21
  163.0 4.9 %weight_rows.5 = bf16[8,384,256]{2,1,0:T(8,128)(2,1)} custom-call(s32[6]{0:T(128)S(1)} %copy-done.8, bf16[16,512,384]{2,1,0:T(8,128)(2,1)S(1)} %bitcast.34, bf16[512,768]{1,0:T(8,128)(2,1)S(1)} %copy-done.5, bf16[8,384,256]{2,1,0:T(8,128)(2,1)S(1)} %collective-permute-done.29.refs_0_), custom_call_target="tpu_custom_call" | custom-call | flops 200000000 | bytes 1000 | tf_op jit(solution)/shard_map/weight_rows/pallas_call | solution.py:278
  170.4 3.9 %collective-permute-start.25 = (f32[8,128]{1,0:T(8,128)S(1)}, f32[8,128]{1,0:T(8,128)S(1)}, u32[]{:S(2)}, u32[]{:S(2)}) collective-permute-start(f32[8,128]{1,0:T(8,128)S(1)} %add.68), channel_id=1, source_target_pairs={{0,8},{1,9},{2,10},{3,11},{4,12},{5,13},{6,14},{7,15},{8,0},{9,1},... | collective-permute-start | bytes 12296 | tf_op jit(solution)/shard_map/ppermute | solution.py:51
  174.3 1.6 collective-permute-done.25
  177.0 3.7 %collective-permute-done.26 = f32[8,128]{1,0:T(8,128)S(1)} collective-permute-done((f32[8,128]{1,0:T(8,128)S(1)}, f32[8,128]{1,0:T(8,128)S(1)}, u32[]{:S(2)}, u32[]{:S(2)}) %collective-permute-start.26) | collective-permute-done | bytes 4128 | tf_op jit(solution)/shard_map/ppermute | solution.py:51
  181.0 3.6 %collective-permute-start.23 = (bf16[512,384]{1,0:T(8,128)(2,1)}, bf16[512,384]{1,0:T(8,128)(2,1)}, u32[]{:S(2)}, u32[]{:S(2)}) collective-permute-start(bf16[512,384]{1,0:T(8,128)(2,1)} %fusion.5), channel_id=1, source_target_pairs={{0,8},{1,9},{2,10},{3,11},{4,12},{5,13},{6,14},{7,15},{8,0},{9,1},... | collective-permute-start | bytes 1179656 | tf_op jit(solution)/shard_map/ppermute | solution.py:51
  185.8 1.8 slice.89
  188.3 6.7 %collective-permute-done.23 = bf16[512,384]{1,0:T(8,128)(2,1)} collective-permute-done((bf16[512,384]{1,0:T(8,128)(2,1)}, bf16[512,384]{1,0:T(8,128)(2,1)}, u32[]{:S(2)}, u32[]{:S(2)}) %collective-permute-start.23) | collective-permute-done | bytes 393248 | tf_op jit(solution)/shard_map/ppermute | solution.py:51
  195.0 2.1 fusion.4
  197.1 20.7 %reduce-scatter.5.cloned.1.call-done.far = bf16[384,256]{1,0:T(8,128)(2,1)} async-done(((bf16[3072,256]{1,0:T(8,128)(2,1)}), bf16[384,256]{1,0:T(8,128)(2,1)}) %reduce-scatter.5.cloned.1.call-update) | async-done | bytes 196624 | tf_op jit(solution)/shard_map/reduce_scatter | solution.py:323
  (117 shorter events, 22.4 us)
Async XLA Ops:
  7.2 178.7 %reduce-scatter.3.cloned.1.call-start = ((), (), s32[]{:S(2)}) async-start(), calls=%async_computation.2 | async-start | bytes 7077888 | tf_op jit(solution)/shard_map/reduce_scatter | solution.py:323
  7.2 12.7 %collective-permute-start.2 = (bf16[512,384]{1,0:T(8,128)(2,1)}, bf16[512,384]{1,0:T(8,128)(2,1)S(1)}, u32[]{:S(2)}, u32[]{:S(2)}) collective-permute-start(bf16[512,384]{1,0:T(8,128)(2,1)} %refs_0_.1), channel_id=1, source_target_pairs={{0,8},{1,9},{2,10},{3,11},{4,12},{5,13},{6,14},{7,15},{8,0},{9,1},... | collective-permute-start | bytes 1179656 | tf_op jit(solution)/shard_map/ppermute | solution.py:51
  8.7 14.8 %collective-permute-start.1 = (bf16[512,384]{1,0:T(8,128)(2,1)}, bf16[512,384]{1,0:T(8,128)(2,1)S(1)}, u32[]{:S(2)}, u32[]{:S(2)}) collective-permute-start(bf16[512,384]{1,0:T(8,128)(2,1)} %refs_0_.1), channel_id=1, source_target_pairs={{0,6},{1,7},{2,0},{3,1},{4,2},{5,3},{6,4},{7,5},{8,14},{9,15},{10,... | collective-permute-start | bytes 1179656 | tf_op jit(solution)/shard_map/ppermute | solution.py:51
  11.7 22.8 %collective-permute-start = (bf16[512,384]{1,0:T(8,128)(2,1)}, bf16[512,384]{1,0:T(8,128)(2,1)S(1)}, u32[]{:S(2)}, u32[]{:S(2)}) collective-permute-start(bf16[512,384]{1,0:T(8,128)(2,1)} %refs_0_.1), channel_id=1, source_target_pairs={{0,2},{1,3},{2,4},{3,5},{4,6},{5,7},{6,0},{7,1},{8,10},{9,11},{10,... | collective-permute-start | bytes 1179656 | tf_op jit(solution)/shard_map/ppermute | solution.py:51
  11.7 22.9 %collective-permute-start.9 = (bf16[512,384]{1,0:T(8,128)(2,1)}, bf16[512,384]{1,0:T(8,128)(2,1)S(1)}, u32[]{:S(2)}, u32[]{:S(2)}) collective-permute-start(bf16[512,384]{1,0:T(8,128)(2,1)} %refs_0_.1), channel_id=1, source_target_pairs={{0,1},{1,0},{2,3},{3,2},{4,5},{5,4},{6,7},{7,6},{8,9},{9,8},{10,11... | collective-permute-start | bytes 1179656 | tf_op jit(solution)/shard_map/ppermute | solution.py:51
  19.9 21.6 %collective-permute-start.3 = (bf16[512,384]{1,0:T(8,128)(2,1)}, bf16[512,384]{1,0:T(8,128)(2,1)S(1)}, u32[]{:S(2)}, u32[]{:S(2)}) collective-permute-start(bf16[512,384]{1,0:T(8,128)(2,1)} %refs_0_.1), channel_id=1, source_target_pairs={{0,4},{1,5},{2,6},{3,7},{4,0},{5,1},{6,2},{7,3},{8,12},{9,13},{10,... | collective-permute-start | bytes 1179656 | tf_op jit(solution)/shard_map/ppermute | solution.py:51
  23.1 14.8 %collective-permute-start.8 = (bf16[256,384]{1,0:T(8,128)(2,1)S(1)}, bf16[256,384]{1,0:T(8,128)(2,1)S(1)}, u32[]{:S(2)}, u32[]{:S(2)}) collective-permute-start(bf16[256,384]{1,0:T(8,128)(2,1)S(1)} %slice.81), channel_id=1, source_target_pairs={{0,4},{1,5},{2,6},{3,7},{4,0},{5,1},{6,2},{7,3},{8,12},{9,13},{10,... | collective-permute-start | bytes 589832 | tf_op jit(solution)/shard_map/ppermute | solution.py:51
  23.5 16.9 %collective-permute-start.6 = (bf16[256,384]{1,0:T(8,128)(2,1)S(1)}, bf16[256,384]{1,0:T(8,128)(2,1)S(1)}, u32[]{:S(2)}, u32[]{:S(2)}) collective-permute-start(bf16[256,384]{1,0:T(8,128)(2,1)S(1)} %slice.81), channel_id=1, source_target_pairs={{0,6},{1,7},{2,0},{3,1},{4,2},{5,3},{6,4},{7,5},{8,14},{9,15},{10,... | collective-permute-start | bytes 589832 | tf_op jit(solution)/shard_map/ppermute | solution.py:51
  34.5 6.9 %collective-permute-start.5 = (bf16[256,384]{1,0:T(8,128)(2,1)S(1)}, bf16[256,384]{1,0:T(8,128)(2,1)S(1)}, u32[]{:S(2)}, u32[]{:S(2)}) collective-permute-start(bf16[256,384]{1,0:T(8,128)(2,1)S(1)} %slice.81), channel_id=1, source_target_pairs={{0,2},{1,3},{2,4},{3,5},{4,6},{5,7},{6,0},{7,1},{8,10},{9,11},{10,... | collective-permute-start | bytes 589832 | tf_op jit(solution)/shard_map/ppermute | solution.py:51
  34.6 12.8 %collective-permute-start.13 = (bf16[512,384]{1,0:T(8,128)(2,1)S(1)}, bf16[512,384]{1,0:T(8,128)(2,1)S(1)}, u32[]{:S(2)}, u32[]{:S(2)}) collective-permute-start(bf16[512,384]{1,0:T(8,128)(2,1)S(1)} %collective-permute-done.2.refs_4_), channel_id=1, source_target_pairs={{0,1},{1,0},{2,3},{3,2},{4,5},{5,4},{6,7},{7,6},{8,9},{9,8},{10,11... | collective-permute-start | bytes 1179656 | tf_op jit(solution)/shard_map/ppermute | solution.py:51
  37.9 11.2 %collective-permute-start.4 = (bf16[512,384]{1,0:T(8,128)(2,1)S(1)}, bf16[512,384]{1,0:T(8,128)(2,1)S(1)}, u32[]{:S(2)}, u32[]{:S(2)}) collective-permute-start(bf16[512,384]{1,0:T(8,128)(2,1)S(1)} %pad_maximum_fusion), channel_id=1, source_target_pairs={{0,8},{1,9},{2,10},{3,11},{4,12},{5,13},{6,14},{7,15},{8,0},{9,1},... | collective-permute-start | bytes 1179656 | tf_op jit(solution)/shard_map/ppermute | solution.py:51
  40.4 1.6 collective-permute-start.18
  41.4 1.4 collective-permute-start.16
  41.4 1.7 collective-permute-start.15
  42.0 11.8 %collective-permute-start.11 = (bf16[512,384]{1,0:T(8,128)(2,1)S(1)}, bf16[512,384]{1,0:T(8,128)(2,1)S(1)}, u32[]{:S(2)}, u32[]{:S(2)}) collective-permute-start(bf16[512,384]{1,0:T(8,128)(2,1)S(1)} %collective-permute-done.1.refs_2_), channel_id=1, source_target_pairs={{0,1},{1,0},{2,3},{3,2},{4,5},{5,4},{6,7},{7,6},{8,9},{9,8},{10,11... | collective-permute-start | bytes 1179656 | tf_op jit(solution)/shard_map/ppermute | solution.py:51
  42.9 11.0 %collective-permute-start.10 = (bf16[512,384]{1,0:T(8,128)(2,1)S(1)}, bf16[512,384]{1,0:T(8,128)(2,1)}, u32[]{:S(2)}, u32[]{:S(2)}) collective-permute-start(bf16[512,384]{1,0:T(8,128)(2,1)S(1)} %collective-permute-done.refs_1_), channel_id=1, source_target_pairs={{0,1},{1,0},{2,3},{3,2},{4,5},{5,4},{6,7},{7,6},{8,9},{9,8},{10,11... | collective-permute-start | bytes 1179656 | tf_op jit(solution)/shard_map/ppermute | solution.py:51
  43.2 10.0 %collective-permute-start.7 = (bf16[256,384]{1,0:T(8,128)(2,1)S(1)}, bf16[256,384]{1,0:T(8,128)(2,1)}, u32[]{:S(2)}, u32[]{:S(2)}) collective-permute-start(bf16[256,384]{1,0:T(8,128)(2,1)S(1)} %slice.82), channel_id=1, source_target_pairs={{0,8},{1,9},{2,10},{3,11},{4,12},{5,13},{6,14},{7,15},{8,0},{9,1},... | collective-permute-start | bytes 589832 | tf_op jit(solution)/shard_map/ppermute | solution.py:51
  47.4 7.5 %collective-permute-start.12 = (bf16[512,384]{1,0:T(8,128)(2,1)S(1)}, bf16[512,384]{1,0:T(8,128)(2,1)}, u32[]{:S(2)}, u32[]{:S(2)}) collective-permute-start(bf16[512,384]{1,0:T(8,128)(2,1)S(1)} %collective-permute-done.3.refs_3_), channel_id=1, source_target_pairs={{0,1},{1,0},{2,3},{3,2},{4,5},{5,4},{6,7},{7,6},{8,9},{9,8},{10,11... | collective-permute-start | bytes 1179656 | tf_op jit(solution)/shard_map/ppermute | solution.py:51
  49.0 5.9 %collective-permute-start.14 = (bf16[512,384]{1,0:T(8,128)(2,1)S(1)}, bf16[512,384]{1,0:T(8,128)(2,1)}, u32[]{:S(2)}, u32[]{:S(2)}) collective-permute-start(bf16[512,384]{1,0:T(8,128)(2,1)S(1)} %collective-permute-done.4.refs_5_), channel_id=1, source_target_pairs={{0,1},{1,0},{2,3},{3,2},{4,5},{5,4},{6,7},{7,6},{8,9},{9,8},{10,11... | collective-permute-start | bytes 1179656 | tf_op jit(solution)/shard_map/ppermute | solution.py:51
  53.1 1.8 collective-permute-start.17
  97.5 120.3 %reduce-scatter.5.cloned.1.call-start = ((), (), s32[]{:S(2)}) async-start(), calls=%async_computation.3 | async-start | bytes 1769472 | tf_op jit(solution)/shard_map/reduce_scatter | solution.py:323
  114.4 7.4 %collective-permute-start.19 = (bf16[8,512,384]{2,1,0:T(8,128)(2,1)S(1)}, bf16[8,512,384]{2,1,0:T(8,128)(2,1)S(1)}, u32[]{:S(2)}, u32[]{:S(2)}) collective-permute-start(bf16[8,512,384]{2,1,0:T(8,128)(2,1)S(1)} %get-tuple-element.24), channel_id=1, source_target_pairs={{0,1},{1,0},{2,3},{3,2},{4,5},{5,4},{6,7},{7,6},{8,9},{9,8},{10,11... | collective-permute-start | bytes 9437192 | tf_op jit(solution)/shard_map/ppermute | solution.py:51
  114.6 48.4 %collective-permute-start.29 = (bf16[8,384,256]{2,1,0:T(8,128)(2,1)S(1)}, bf16[8,384,256]{2,1,0:T(8,128)(2,1)S(1)}, u32[]{:S(2)}, u32[]{:S(2)}) collective-permute-start(bf16[8,384,256]{2,1,0:T(8,128)(2,1)S(1)} %weight_rows.4), channel_id=1, source_target_pairs={{0,128},{1,129},{2,130},{3,131},{4,132},{5,133},{6,134},{7,135},{8... | collective-permute-start | bytes 4718600 | tf_op jit(solution)/shard_map/ppermute | solution.py:51
  122.4 21.3 %collective-permute-start.20 = (bf16[2,512,384]{2,1,0:T(8,128)(2,1)S(1)}, bf16[2,512,384]{2,1,0:T(8,128)(2,1)S(1)}, u32[]{:S(2)}, u32[]{:S(2)}) collective-permute-start(bf16[2,512,384]{2,1,0:T(8,128)(2,1)S(1)} %get-tuple-element.33), channel_id=1, source_target_pairs={{0,2},{1,3},{2,4},{3,5},{4,6},{5,7},{6,0},{7,1},{8,10},{9,11},{10,... | collective-permute-start | bytes 2359304 | tf_op jit(solution)/shard_map/ppermute | solution.py:51
  122.7 37.2 %collective-permute-start.22 = (bf16[2,512,384]{2,1,0:T(8,128)(2,1)S(1)}, bf16[2,512,384]{2,1,0:T(8,128)(2,1)S(1)}, u32[]{:S(2)}, u32[]{:S(2)}) collective-permute-start(bf16[2,512,384]{2,1,0:T(8,128)(2,1)S(1)} %get-tuple-element.34), channel_id=1, source_target_pairs={{0,6},{1,7},{2,0},{3,1},{4,2},{5,3},{6,4},{7,5},{8,14},{9,15},{10,... | collective-permute-start | bytes 2359304 | tf_op jit(solution)/shard_map/ppermute | solution.py:51
  126.0 35.7 %collective-permute-start.21 = (bf16[2,512,384]{2,1,0:T(8,128)(2,1)S(1)}, bf16[2,512,384]{2,1,0:T(8,128)(2,1)S(1)}, u32[]{:S(2)}, u32[]{:S(2)}) collective-permute-start(bf16[2,512,384]{2,1,0:T(8,128)(2,1)S(1)} %get-tuple-element.35), channel_id=1, source_target_pairs={{0,4},{1,5},{2,6},{3,7},{4,0},{5,1},{6,2},{7,3},{8,12},{9,13},{10,... | collective-permute-start | bytes 2359304 | tf_op jit(solution)/shard_map/ppermute | solution.py:51
  169.2 1.3 collective-permute-start.24
  170.4 5.5 %collective-permute-start.25 = (f32[8,128]{1,0:T(8,128)S(1)}, f32[8,128]{1,0:T(8,128)S(1)}, u32[]{:S(2)}, u32[]{:S(2)}) collective-permute-start(f32[8,128]{1,0:T(8,128)S(1)} %add.68), channel_id=1, source_target_pairs={{0,8},{1,9},{2,10},{3,11},{4,12},{5,13},{6,14},{7,15},{8,0},{9,1},... | collective-permute-start | bytes 12296 | tf_op jit(solution)/shard_map/ppermute | solution.py:51
  175.9 4.8 %collective-permute-start.26 = (f32[8,128]{1,0:T(8,128)S(1)}, f32[8,128]{1,0:T(8,128)S(1)}, u32[]{:S(2)}, u32[]{:S(2)}) collective-permute-start(f32[8,128]{1,0:T(8,128)S(1)} %add.69), channel_id=1, source_target_pairs={{0,2},{1,3},{2,4},{3,5},{4,6},{5,7},{6,0},{7,1},{8,10},{9,11},{10,... | collective-permute-start | bytes 12296 | tf_op jit(solution)/shard_map/ppermute | solution.py:51
  180.7 5.1 %collective-permute-start.27 = (f32[8,128]{1,0:T(8,128)S(1)}, f32[8,128]{1,0:T(8,128)S(1)}, u32[]{:S(2)}, u32[]{:S(2)}) collective-permute-start(f32[8,128]{1,0:T(8,128)S(1)} %add.70), channel_id=1, source_target_pairs={{0,4},{1,5},{2,6},{3,7},{4,0},{5,1},{6,2},{7,3},{8,12},{9,13},{10,... | collective-permute-start | bytes 12296 | tf_op jit(solution)/shard_map/ppermute | solution.py:51
  181.0 14.0 %collective-permute-start.23 = (bf16[512,384]{1,0:T(8,128)(2,1)}, bf16[512,384]{1,0:T(8,128)(2,1)}, u32[]{:S(2)}, u32[]{:S(2)}) collective-permute-start(bf16[512,384]{1,0:T(8,128)(2,1)} %fusion.5), channel_id=1, source_target_pairs={{0,8},{1,9},{2,10},{3,11},{4,12},{5,13},{6,14},{7,15},{8,0},{9,1},... | collective-permute-start | bytes 1179656 | tf_op jit(solution)/shard_map/ppermute | solution.py:51
  187.7 30.1 %collective-permute-start.28 = (bf16[384,512]{1,0:T(8,128)(2,1)}, bf16[384,512]{1,0:T(8,128)(2,1)S(1)}, u32[]{:S(2)}, u32[]{:S(2)}) collective-permute-start(bf16[384,512]{1,0:T(8,128)(2,1)} %slice.89), channel_id=1, source_target_pairs={{0,128},{1,129},{2,130},{3,131},{4,132},{5,133},{6,134},{7,135},{8... | collective-permute-start | bytes 1179656 | tf_op jit(solution)/shard_map/ppermute | solution.py:51
  (27 other events, 394.1 us)
Sparse Core Ops, SparseCore 0:
  97.6 78.5 reduce-scatter.2
  178.8 38.9 reduce-scatter.4
where the time goes:
time: 227 us; the launch traced here: 226 us
  waiting for transfers between devices  98.4 us (43%)
  Pallas kernels  56.9 us (25%)
  starting transfers between devices  33.5 us (15%)
  local copies, waits for them, and re-layouts  19.7 us (9%)
  between operations  14.4 us (6%)
  other arithmetic  3.55 us (2%)
    ppermute x30, waiting for transfers between devices, send(): return lax.ppermute(value, AXES, pairs)  77.7 us
    ppermute x30, starting transfers between devices, send(): return lax.ppermute(value, AXES, pairs)  33.4 us
    pallas_call x1, Pallas kernels, front(): pl.pallas_call(front_kernel, out_shape=(jax.ShapeDtypeStruct((TOK, COLS),...  28.6 us
    reduce_scatter x2, waiting for transfers between devices, sum_over_z(): lax.psum_scatter(rows, 'dp', scatter_dimension=0, tiled=True, axis_index_...  20.7 us
    unnamed x54, local copies, waits for them, and re-layouts  16 us
    pallas_call x3, Pallas kernels, weight_rows(): pl.pallas_call(functools.partial(rows_kernel, far is not None), grid_spec...  15.3 us
    pallas_call x2, Pallas kernels, back(): pl.pallas_call(back_kernel, grid_spec=pltpu.PrefetchScalarGridSpec(num_sc...  12.1 us
  transfers between devices with their start and end apart: 32, of which 19 were waited for; matrix products, arithmetic and copies ran while one was open for 3% of the time, Pallas kernels for 9%

commit v1 on v0

--- a/solution.py
+++ b/solution.py
@@ -55,35 +55,16 @@
     return lax.optimization_barrier((value, *first))[0]
 
 
-PIECES = (
-    (0, 0, 0, 512, 0, 0),
-    (1, 0, 0, 512, 0, 3),
-    (2, 0, 0, 512, 0, 1),
-    (3, 0, 0, 512, 0, 2),
-    (4, 0, 0, 512, 1, 0),
-    (5, 0, 256, 256, 1, 3),
-    (5, 256, 256, 256, 1, 1),
-    (6, 0, 0, 256, 1, 3),
-    (7, 0, 0, 256, 1, 1),
-    (8, 0, 256, 256, 1, 2),
-    (9, 0, 0, 256, 1, 2),
-)
-N_MSG = 10
-N_COPY = 2 * len(PIECES)
+PIECES = ((0, 0), (0, 3), (0, 1), (1, 0), (1, 3), (1, 1), (0, 2), (1, 2))
+N_MSG = 8
 
 
 def gather_tokens(own):
     x = send(own, xh=1)
     a = send(own, y=1)
     b = send(own, y=-1)
-    d = send(after(own, x), y=2)
-    ab = send(jnp.concatenate([a[256:], b[256:]]), xh=1)
-    low = x[:256]
-    xa = send(low, y=1)
-    xb = send(low, y=-1)
-    xd = send(low, y=2)
-    dx = send(d[256:], xh=1)
-    mine = [own, a, b, d, x, ab, xa, xb, dx, xd]
+    held = after(own, x, a, b)
+    mine = [own, a, b, x, send(a, xh=1), send(b, xh=1), send(held, y=2), send(x, y=2)]
     return mine + [send(m, core=1) for m in mine]
 
 
@@ -109,17 +90,12 @@
     xs, w, proj, w_sem, x_sem, b_sem = refs[2 * N_MSG + 7 :]
     x_hi, y, core = sc[0], sc[1], sc[2]
     copies = []
-    for i in range(N_COPY):
-        other, (m, src, row, rows, dx, dy) = i // len(PIECES), PIECES[i % len(PIECES)]
-        block = lax.rem(x_hi + dx, 2) * 8 + lax.rem(y + dy, 4) * 2 + lax.rem(core + other, 2)
+    for m in range(2 * N_MSG):
+        dx, dy = PIECES[m % N_MSG]
+        c = lax.rem(core + m // N_MSG, 2)
+        block = lax.rem(x_hi + dx, 2) * 8 + lax.rem(y + dy, 4) * 2 + c
         at = pl.ds(pl.multiple_of(block * OWN, OWN), OWN)
-        copies.append(
-            pltpu.make_async_copy(
-                msgs[other * N_MSG + m].at[pl.ds(src, rows)],
-                xs.at[pl.ds(row, rows), at],
-                x_sem.at[i],
-            )
-        )
+        copies.append(pltpu.make_async_copy(msgs[m], xs.at[:, at], x_sem.at[m]))
     loads = [pltpu.make_async_copy(w_hbm.at[s], w.at[s], w_sem.at[s]) for s in range(3)]
     for copy in copies + loads:
         copy.start()
@@ -211,7 +187,7 @@
             pltpu.VMEM((3, D, COLS), BF),
             pltpu.VMEM((TOK, 3 * COLS), F32),
             pltpu.SemaphoreType.DMA((3,)),
-            pltpu.SemaphoreType.DMA((N_COPY,)),
+            pltpu.SemaphoreType.DMA((2 * N_MSG,)),
             pltpu.SemaphoreType.DMA((N_MP,)),
         ],
         compiler_params=params(),
@@ -260,6 +236,15 @@
     )(sc, d_proj, w)
 
 
+HOPS = (4, -3, 3, -2, 2, -1, 1, 0)
+
+
+def by_hop(s, i):
+    away = 4 - lax.div(i, 2)
+    hop = jnp.where(i == 7, 0, jnp.where(lax.rem(i, 2) == 0, away, 1 - away))
+    return lax.rem(s[4] + (1 - 2 * s[2]) * hop + 8, 8)
+
+
 def rows_kernel(with_far, sc, n, d, *refs):
     rows = dot(n[0], d[...], ((0,), (0,)))
     if with_far:
@@ -272,8 +257,9 @@
     n_sides = len(sides)
 
     def block(i, s):
-        side = lax.rem(i, 2) if n_sides == 2 else sides[0]
-        return (lax.rem(s[3] + side, 2) * 8 + i // n_sides, 0, 0)
+        if n_sides == 2:
+            return (lax.rem(s[3] + lax.rem(i, 2), 2) * 8 + lax.div(i, 2), 0, 0)
+        return (lax.rem(s[3] + sides[0], 2) * 8 + by_hop(s, i), 0, 0)
 
     return pl.pallas_call(
         functools.partial(rows_kernel, far is not None),
@@ -288,7 +274,7 @@
             out_specs=chunk(),
         ),
         out_shape=jax.ShapeDtypeStruct((8 * n_sides, OWN, width), BF),
-        compiler_params=params(20),
+        compiler_params=params(60 if n_sides == 2 else 20),
         cost_estimate=cost(2.0 * n_sides),
         name="weight_rows",
     )(sc, blocks, d_proj, *([] if far is None else [far]))
@@ -352,12 +338,18 @@
     for shift in ({"core": 1}, {"xh": 1}, {"y": 1}, {"y": 2}):
         sums = sums + send(sums, **shift)
     over_y = sum(o.astype(F32) for o in over_y)
-    across = over_y[1].astype(BF)
+    across = after(over_y[1].astype(BF), sums)
     d_late = after(d_proj, across)
     across = send(across, xh=1)
 
     second = weight_rows(sc, blocks, d_late, COLS, 2, (0,), far)
-    second = sum_over_z(second)
+    add = lambda *rows: sum(r.astype(F32) for r in rows).astype(BF)
+    long, short = send(second[0], turn=True, z=1), send(second[1], turn=True, z=-1)
+    for i in range(1, 4):
+        long = send(add(long, second[2 * i]), turn=True, z=1)
+        if i < 3:
+            short = send(add(short, second[2 * i + 1]), turn=True, z=-1)
+    second = add(long, short, second[7])
     grad_w = grad_rows(first, send(first[OWN:], xl=1), second)
     grad_w = jnp.transpose(grad_w, (1, 0, 2))
 

time: 227 us -> 233 us (1.026)
  waiting for transfers between devices: 98.4 us -> 79.5 us
  starting transfers between devices: 33.5 us -> 45.7 us
  Pallas kernels: 56.9 us -> 65.3 us
  other arithmetic: 3.55 us -> 8.2 us
    reduce_scatter x2 -> x1, waiting for transfers between devices: 20.7 us -> 0.01 us  [sum_over_z(): lax.psum_scatter(rows, 'dp', scatter_dimension=0, tiled=True, axis_index_...]
    ppermute x30 -> x33, starting transfers between devices: 33.4 us -> 45.6 us  [send(): return lax.ppermute(value, AXES, pairs)]
    pallas_call x3, Pallas kernels: 15.3 us -> 22.9 us  [weight_rows(): pl.pallas_call(functools.partial(rows_kernel, far is not None), grid_spec...]
    ppermute x30 -> x33, waiting for transfers between devices: 77.7 us -> 79.4 us  [send(): return lax.ppermute(value, AXES, pairs)]
    unnamed x54 -> x46, local copies, waits for them, and re-layouts: 16 us -> 15.7 us
  transfers between devices with their start and end apart: 32 -> 34, of which waited for: 19 -> 16; matrix products, arithmetic and copies ran while one was open for 3% -> 4% of each run, Pallas kernels for 9% -> 9%
where the time goes in v1:
time: 233 us; the launch traced here: 231 us
  waiting for transfers between devices  79.5 us (34%)
  Pallas kernels  65.3 us (28%)
  starting transfers between devices  45.7 us (20%)
  local copies, waits for them, and re-layouts  17.7 us (8%)
  between operations  14.4 us (6%)
  other arithmetic  8.2 us (4%)
    ppermute x33, waiting for transfers between devices, send(): return lax.ppermute(value, AXES, pairs)  79.4 us
    ppermute x33, starting transfers between devices, send(): return lax.ppermute(value, AXES, pairs)  45.6 us
    pallas_call x1, Pallas kernels, front(): pl.pallas_call(front_kernel, out_shape=(jax.ShapeDtypeStruct((TOK, COLS),...  29.5 us
    pallas_call x3, Pallas kernels, weight_rows(): pl.pallas_call(functools.partial(rows_kernel, far is not None), grid_spec...  22.9 us
    unnamed x46, local copies, waits for them, and re-layouts  15.7 us
    pallas_call x2, Pallas kernels, back(): pl.pallas_call(back_kernel, grid_spec=pltpu.PrefetchScalarGridSpec(num_sc...  12.1 us
  transfers between devices with their start and end apart: 34, of which 16 were waited for; matrix products, arithmetic and copies ran while one was open for 4% of the time, Pallas kernels for 9%

profile of v1, /device:TPU:6, one launch (start us, length us, event | category | flops | bytes accessed | tf_op | source)
XLA Modules:
  0.0 230.8 jit_solution(17008864314764136306)
XLA Ops:
  8.7 3.0 %collective-permute-start.1 = (bf16[512,384]{1,0:T(8,128)(2,1)}, bf16[512,384]{1,0:T(8,128)(2,1)S(1)}, u32[]{:S(2)}, u32[]{:S(2)}) collective-permute-start(bf16[512,384]{1,0:T(8,128)(2,1)} %refs_0_.1), channel_id=1, source_target_pairs={{0,6},{1,7},{2,0},{3,1},{4,2},{5,3},{6,4},{7,5},{8,14},{9,15},{10,... | collective-permute-start | bytes 1179656 | tf_op jit(solution)/shard_map/ppermute | solution.py:51
  11.7 8.1 %collective-permute-done.2.refs_3_ = bf16[512,384]{1,0:T(8,128)(2,1)S(1)} collective-permute-done((bf16[512,384]{1,0:T(8,128)(2,1)}, bf16[512,384]{1,0:T(8,128)(2,1)S(1)}, u32[]{:S(2)}, u32[]{:S(2)}) %collective-permute-start.2) | collective-permute-done | bytes 393248 | tf_op jit(solution)/shard_map/ppermute | solution.py:51
  19.9 3.2 %collective-permute-start.6 = (bf16[512,384]{1,0:T(8,128)(2,1)S(1)}, bf16[512,384]{1,0:T(8,128)(2,1)S(1)}, u32[]{:S(2)}, u32[]{:S(2)}) collective-permute-start(bf16[512,384]{1,0:T(8,128)(2,1)S(1)} %collective-permute-done.2.refs_3_), channel_id=1, source_target_pairs={{0,4},{1,5},{2,6},{3,7},{4,0},{5,1},{6,2},{7,3},{8,12},{9,13},{10,... | collective-permute-start | bytes 1179656 | tf_op jit(solution)/shard_map/ppermute | solution.py:51
  27.3 6.0 %collective-permute-done.6.refs_7_ = bf16[512,384]{1,0:T(8,128)(2,1)S(1)} collective-permute-done((bf16[512,384]{1,0:T(8,128)(2,1)S(1)}, bf16[512,384]{1,0:T(8,128)(2,1)S(1)}, u32[]{:S(2)}, u32[]{:S(2)}) %collective-permute-start.6) | collective-permute-done | bytes 393248 | tf_op jit(solution)/shard_map/ppermute | solution.py:51
  33.8 3.0 %collective-permute-done.4.refs_5_ = bf16[512,384]{1,0:T(8,128)(2,1)S(1)} collective-permute-done((bf16[512,384]{1,0:T(8,128)(2,1)S(1)}, bf16[512,384]{1,0:T(8,128)(2,1)S(1)}, u32[]{:S(2)}, u32[]{:S(2)}) %collective-permute-start.4) | collective-permute-done | bytes 393248 | tf_op jit(solution)/shard_map/ppermute | solution.py:51
  36.9 4.5 %collective-permute-done.5.refs_6_ = bf16[512,384]{1,0:T(8,128)(2,1)S(1)} collective-permute-done((bf16[512,384]{1,0:T(8,128)(2,1)}, bf16[512,384]{1,0:T(8,128)(2,1)S(1)}, u32[]{:S(2)}, u32[]{:S(2)}) %collective-permute-start.5) | collective-permute-done | bytes 393248 | tf_op jit(solution)/shard_map/ppermute | solution.py:51
  41.3 3.7 %collective-permute-done.3.refs_4_ = bf16[512,384]{1,0:T(8,128)(2,1)} collective-permute-done((bf16[512,384]{1,0:T(8,128)(2,1)S(1)}, bf16[512,384]{1,0:T(8,128)(2,1)}, u32[]{:S(2)}, u32[]{:S(2)}) %collective-permute-start.3) | collective-permute-done | bytes 393248 | tf_op jit(solution)/shard_map/ppermute | solution.py:51
  47.1 29.5 %front.1 = (bf16[512,256]{1,0:T(8,128)(2,1)}, bf16[512,768]{1,0:T(8,128)(2,1)}, bf16[16,512,384]{2,1,0:T(8,128)(2,1)}, f32[512,128]{1,0:T(8,128)}, f32[512,128]{1,0:T(8,128)}) custom-call(s32[6]{0:T(128)} %stack.36.sc, bf16[512,384]{1,0:T(8,128)(2,1)} %refs_0_.1, bf16[512,384]{1,0:T(8,128)(2,1)} %copy-done.15, bf16[512,384]{1,0:T(8,128)(2,1)} %copy-done.14, ...), custom_call_target="tpu_custom_call" | custom-call | flops 2500000000 | bytes 1000 | tf_op jit(solution)/shard_map/front/pallas_call | solution.py:174
  76.6 14.7 %weight_rows.3 = bf16[16,384,512]{2,1,0:T(8,128)(2,1)} custom-call(s32[6]{0:T(128)} %stack.36.sc, bf16[16,512,384]{2,1,0:T(8,128)(2,1)} %get-tuple-element.22.n, bf16[512,768]{1,0:T(8,128)(2,1)} %get-tuple-element.32.d.d_proj), custom_call_target="tpu_custom_call" | custom-call | flops 400000000 | bytes 1000 | tf_op jit(solution)/shard_map/weight_rows/pallas_call | solution.py:264
  92.5 2.8 %copy-done.1 = bf16[16,512,384]{2,1,0:T(8,128)(2,1)S(1)} copy-done((bf16[16,512,384]{2,1,0:T(8,128)(2,1)S(1)}, bf16[16,512,384]{2,1,0:T(8,128)(2,1)}, u32[]{:S(2)}) %copy-start.1) | copy-done | bytes 6291480
  95.2 4.9 %weight_rows.4 = bf16[8,384,256]{2,1,0:T(8,128)(2,1)} custom-call(s32[6]{0:T(128)S(1)} %copy-done.8, bf16[16,512,384]{2,1,0:T(8,128)(2,1)S(1)} %copy-done.1, bf16[512,768]{1,0:T(8,128)(2,1)S(1)} %copy-done.3), custom_call_target="tpu_custom_call" | custom-call | flops 200000000 | bytes 1000 | tf_op jit(solution)/shard_map/weight_rows/pallas_call | solution.py:264
  100.2 3.7 %copy-done = bf16[6144,3,256]{2,0,1:T(8,128)(2,1)S(1)} copy-done((bf16[6144,3,256]{2,0,1:T(8,128)(2,1)S(1)}, bf16[6144,3,256]{2,0,1:T(8,128)(2,1)}, u32[]{:S(2)}) %copy-start) | copy-done | bytes 9437208
  103.9 6.1 %back.2 = (bf16[8,512,384]{2,1,0:T(8,128)(2,1)S(1)}, f32[512,128]{1,0:T(8,128)S(1)}) custom-call(s32[6]{0:T(128)S(1)} %copy-done.8, bf16[512,768]{1,0:T(8,128)(2,1)S(1)} %copy-done.3, bf16[3,6144,256]{2,1,0:T(8,128)(2,1)S(1)} %bitcast.64), custom_call_target="tpu_custom_call" | custom-call | flops 600000000 | bytes 1000 | tf_op jit(solution)/shard_map/back/pallas_call | solution.py:215
  110.2 8.4 %collective-permute-start.25 = (bf16[8,384,256]{2,1,0:T(8,128)(2,1)}, bf16[8,384,256]{2,1,0:T(8,128)(2,1)S(1)}, u32[]{:S(2)}, u32[]{:S(2)}) collective-permute-start(bf16[8,384,256]{2,1,0:T(8,128)(2,1)} %weight_rows.4), channel_id=1, source_target_pairs={{0,128},{1,129},{2,130},{3,131},{4,132},{5,133},{6,134},{7,135},{8... | collective-permute-start | bytes 4718600 | tf_op jit(solution)/shard_map/ppermute | solution.py:51
  118.6 6.0 %back.3 = (bf16[8,512,384]{2,1,0:T(8,128)(2,1)S(1)}, f32[512,128]{1,0:T(8,128)S(1)}) custom-call(s32[6]{0:T(128)S(1)} %copy-done.8, bf16[512,768]{1,0:T(8,128)(2,1)S(1)} %copy-done.3, bf16[3,6144,256]{2,1,0:T(8,128)(2,1)S(1)} %bitcast.65), custom_call_target="tpu_custom_call" | custom-call | flops 600000000 | bytes 1000 | tf_op jit(solution)/shard_map/back/pallas_call | solution.py:215
  128.0 3.2 %collective-permute-start.18 = (bf16[2,512,384]{2,1,0:T(8,128)(2,1)}, bf16[2,512,384]{2,1,0:T(8,128)(2,1)}, u32[]{:S(2)}, u32[]{:S(2)}) collective-permute-start(bf16[2,512,384]{2,1,0:T(8,128)(2,1)} %get-tuple-element.38), channel_id=1, source_target_pairs={{0,6},{1,7},{2,0},{3,1},{4,2},{5,3},{6,4},{7,5},{8,14},{9,15},{10,... | collective-permute-start | bytes 2359304 | tf_op jit(solution)/shard_map/ppermute | solution.py:51
  132.8 4.1 %collective-permute-start.20 = (f32[8,128]{1,0:T(8,128)S(1)}, f32[8,128]{1,0:T(8,128)S(1)}, u32[]{:S(2)}, u32[]{:S(2)}) collective-permute-start(f32[8,128]{1,0:T(8,128)S(1)} %add.86), channel_id=1, source_target_pairs={{0,8},{1,9},{2,10},{3,11},{4,12},{5,13},{6,14},{7,15},{8,0},{9,1},... | collective-permute-start | bytes 12296 | tf_op jit(solution)/shard_map/ppermute | solution.py:51
  136.9 20.7 %collective-permute-done.20 = f32[8,128]{1,0:T(8,128)S(1)} collective-permute-done((f32[8,128]{1,0:T(8,128)S(1)}, f32[8,128]{1,0:T(8,128)S(1)}, u32[]{:S(2)}, u32[]{:S(2)}) %collective-permute-start.20) | collective-permute-done | bytes 4128 | tf_op jit(solution)/shard_map/ppermute | solution.py:51
  157.7 8.4 %collective-permute-done.21 = f32[8,128]{1,0:T(8,128)S(1)} collective-permute-done((f32[8,128]{1,0:T(8,128)S(1)}, f32[8,128]{1,0:T(8,128)S(1)}, u32[]{:S(2)}, u32[]{:S(2)}) %collective-permute-start.21) | collective-permute-done | bytes 4128 | tf_op jit(solution)/shard_map/ppermute | solution.py:51
  166.0 5.1 %collective-permute-done.22 = f32[8,128]{1,0:T(8,128)S(1)} collective-permute-done((f32[8,128]{1,0:T(8,128)S(1)}, f32[8,128]{1,0:T(8,128)S(1)}, u32[]{:S(2)}, u32[]{:S(2)}) %collective-permute-start.22) | collective-permute-done | bytes 4128 | tf_op jit(solution)/shard_map/ppermute | solution.py:51
  171.2 2.6 %convert_add_fusion = f32[2,512,384]{2,1,0:T(8,128)S(1)} fusion(bf16[2,512,384]{2,1,0:T(8,128)(2,1)} %collective-permute-done.18, bf16[2,512,384]{2,1,0:T(8,128)(2,1)} %collective-permute-done.17, bf16[2,512,384]{2,1,0:T(8,128)(2,1)} %collective-permute-done.16, bf16[8,512,384]{2,1,0:T(8,128)(2,1)} %copy-done.10, bf16[8,512,384]{2,1,0:T(8,128)(2,1)} %copy-done.4), kind=kLoop, calls=%fused_computation | loop fusion | flops 4325376 | bytes 5505024 | tf_op jit(solution)/shard_map/add | solution.py:340
  176.1 2.8 %copy-done.2 = bf16[16,512,384]{2,1,0:T(8,128)(2,1)S(1)} copy-done((bf16[16,512,384]{2,1,0:T(8,128)(2,1)S(1)}, bf16[16,512,384]{2,1,0:T(8,128)(2,1)}, u32[]{:S(2)}) %copy-start.2) | copy-done | bytes 6291480
  180.3 3.2 %weight_rows.5 = bf16[8,384,256]{2,1,0:T(8,128)(2,1)S(1)} custom-call(s32[6]{0:T(128)S(1)} %copy-done.8, bf16[16,512,384]{2,1,0:T(8,128)(2,1)S(1)} %copy-done.2, bf16[512,768]{1,0:T(8,128)(2,1)S(1)} %copy-done.3, bf16[8,384,256]{2,1,0:T(8,128)(2,1)S(1)} %copy-done.7), custom_call_target="tpu_custom_call" | custom-call | flops 200000000 | bytes 1000 | tf_op jit(solution)/shard_map/weight_rows/pallas_call | solution.py:264
  183.5 2.3 collective-permute-start.26
  185.8 3.9 %collective-permute-start.30 = (bf16[384,256]{1,0:T(8,128)(2,1)S(1)}, bf16[384,256]{1,0:T(8,128)(2,1)S(1)}, u32[]{:S(2)}, u32[]{:S(2)}) collective-permute-start(bf16[384,256]{1,0:T(8,128)(2,1)S(1)} %get-tuple-element.45), channel_id=1, source_target_pairs={{0,112},{1,17},{2,114},{3,19},{4,116},{5,21},{6,118},{7,23},{8,120... | collective-permute-start | bytes 589832 | tf_op jit(solution)/shard_map/ppermute | solution.py:51
  189.7 5.5 %collective-permute-done.26 = bf16[384,256]{1,0:T(8,128)(2,1)S(1)} collective-permute-done((bf16[384,256]{1,0:T(8,128)(2,1)S(1)}, bf16[384,256]{1,0:T(8,128)(2,1)S(1)}, u32[]{:S(2)}, u32[]{:S(2)}) %collective-permute-start.26) | collective-permute-done | bytes 196640 | tf_op jit(solution)/shard_map/ppermute | solution.py:51
  195.6 3.5 %collective-permute-start.23 = (bf16[512,384]{1,0:T(8,128)(2,1)S(1)}, bf16[512,384]{1,0:T(8,128)(2,1)S(1)}, u32[]{:S(2)}, u32[]{:S(2)}) collective-permute-start(bf16[512,384]{1,0:T(8,128)(2,1)S(1)} %fusion.5), channel_id=1, source_target_pairs={{0,8},{1,9},{2,10},{3,11},{4,12},{5,13},{6,14},{7,15},{8,0},{9,1},... | collective-permute-start | bytes 1179656 | tf_op jit(solution)/shard_map/ppermute | solution.py:51
  199.2 3.0 %collective-permute-done.27 = bf16[384,256]{1,0:T(8,128)(2,1)S(1)} collective-permute-done((bf16[384,256]{1,0:T(8,128)(2,1)S(1)}, bf16[384,256]{1,0:T(8,128)(2,1)S(1)}, u32[]{:S(2)}, u32[]{:S(2)}) %collective-permute-start.27) | collective-permute-done | bytes 196640 | tf_op jit(solution)/shard_map/ppermute | solution.py:51
  202.4 3.2 %collective-permute-start.31 = (bf16[384,256]{1,0:T(8,128)(2,1)S(1)}, bf16[384,256]{1,0:T(8,128)(2,1)S(1)}, u32[]{:S(2)}, u32[]{:S(2)}) collective-permute-start(bf16[384,256]{1,0:T(8,128)(2,1)S(1)} %get-tuple-element.43), channel_id=1, source_target_pairs={{0,112},{1,17},{2,114},{3,19},{4,116},{5,21},{6,118},{7,23},{8,120... | collective-permute-start | bytes 589832 | tf_op jit(solution)/shard_map/ppermute | solution.py:51
  205.6 3.6 %collective-permute-done.28 = bf16[384,256]{1,0:T(8,128)(2,1)S(1)} collective-permute-done((bf16[384,256]{1,0:T(8,128)(2,1)S(1)}, bf16[384,256]{1,0:T(8,128)(2,1)S(1)}, u32[]{:S(2)}, u32[]{:S(2)}) %collective-permute-start.28) | collective-permute-done | bytes 196640 | tf_op jit(solution)/shard_map/ppermute | solution.py:51
  210.3 3.8 %collective-permute-start.32 = (bf16[384,256]{1,0:T(8,128)(2,1)S(1)}, bf16[384,256]{1,0:T(8,128)(2,1)}, u32[]{:S(2)}, u32[]{:S(2)}) collective-permute-start(bf16[384,256]{1,0:T(8,128)(2,1)S(1)} %get-tuple-element.41), channel_id=1, source_target_pairs={{0,112},{1,17},{2,114},{3,19},{4,116},{5,21},{6,118},{7,23},{8,120... | collective-permute-start | bytes 589832 | tf_op jit(solution)/shard_map/ppermute | solution.py:51
  219.1 3.9 %collective-permute-done.24.other = bf16[384,512]{1,0:T(8,128)(2,1)S(1)} collective-permute-done((bf16[384,512]{1,0:T(8,128)(2,1)S(1)}, bf16[384,512]{1,0:T(8,128)(2,1)S(1)}, u32[]{:S(2)}, u32[]{:S(2)}) %collective-permute-start.24) | collective-permute-done | bytes 393248 | tf_op jit(solution)/shard_map/ppermute | solution.py:51
  (111 shorter events, 25.9 us)
Async XLA Ops:
  7.2 206.9 %reduce-scatter.2.cloned.1.call-start = ((), (), s32[]{:S(2)}) async-start(), calls=%async_computation.1 | async-start | bytes 7077888 | tf_op jit(solution)/shard_map/reduce_scatter | solution.py:309
  7.2 12.7 %collective-permute-start.2 = (bf16[512,384]{1,0:T(8,128)(2,1)}, bf16[512,384]{1,0:T(8,128)(2,1)S(1)}, u32[]{:S(2)}, u32[]{:S(2)}) collective-permute-start(bf16[512,384]{1,0:T(8,128)(2,1)} %refs_0_.1), channel_id=1, source_target_pairs={{0,8},{1,9},{2,10},{3,11},{4,12},{5,13},{6,14},{7,15},{8,0},{9,1},... | collective-permute-start | bytes 1179656 | tf_op jit(solution)/shard_map/ppermute | solution.py:51
  8.7 14.4 %collective-permute-start.1 = (bf16[512,384]{1,0:T(8,128)(2,1)}, bf16[512,384]{1,0:T(8,128)(2,1)S(1)}, u32[]{:S(2)}, u32[]{:S(2)}) collective-permute-start(bf16[512,384]{1,0:T(8,128)(2,1)} %refs_0_.1), channel_id=1, source_target_pairs={{0,6},{1,7},{2,0},{3,1},{4,2},{5,3},{6,4},{7,5},{8,14},{9,15},{10,... | collective-permute-start | bytes 1179656 | tf_op jit(solution)/shard_map/ppermute | solution.py:51
  11.7 11.7 %collective-permute-start = (bf16[512,384]{1,0:T(8,128)(2,1)}, bf16[512,384]{1,0:T(8,128)(2,1)S(1)}, u32[]{:S(2)}, u32[]{:S(2)}) collective-permute-start(bf16[512,384]{1,0:T(8,128)(2,1)} %refs_0_.1), channel_id=1, source_target_pairs={{0,2},{1,3},{2,4},{3,5},{4,6},{5,7},{6,0},{7,1},{8,10},{9,11},{10,... | collective-permute-start | bytes 1179656 | tf_op jit(solution)/shard_map/ppermute | solution.py:51
  11.7 13.8 %collective-permute-start.7 = (bf16[512,384]{1,0:T(8,128)(2,1)}, bf16[512,384]{1,0:T(8,128)(2,1)S(1)}, u32[]{:S(2)}, u32[]{:S(2)}) collective-permute-start(bf16[512,384]{1,0:T(8,128)(2,1)} %refs_0_.1), channel_id=1, source_target_pairs={{0,1},{1,0},{2,3},{3,2},{4,5},{5,4},{6,7},{7,6},{8,9},{9,8},{10,11... | collective-permute-start | bytes 1179656 | tf_op jit(solution)/shard_map/ppermute | solution.py:51
  19.9 5.7 %collective-permute-start.10 = (bf16[512,384]{1,0:T(8,128)(2,1)S(1)}, bf16[512,384]{1,0:T(8,128)(2,1)S(1)}, u32[]{:S(2)}, u32[]{:S(2)}) collective-permute-start(bf16[512,384]{1,0:T(8,128)(2,1)S(1)} %collective-permute-done.2.refs_3_), channel_id=1, source_target_pairs={{0,1},{1,0},{2,3},{3,2},{4,5},{5,4},{6,7},{7,6},{8,9},{9,8},{10,11... | collective-permute-start | bytes 1179656 | tf_op jit(solution)/shard_map/ppermute | solution.py:51
  19.9 13.4 %collective-permute-start.6 = (bf16[512,384]{1,0:T(8,128)(2,1)S(1)}, bf16[512,384]{1,0:T(8,128)(2,1)S(1)}, u32[]{:S(2)}, u32[]{:S(2)}) collective-permute-start(bf16[512,384]{1,0:T(8,128)(2,1)S(1)} %collective-permute-done.2.refs_3_), channel_id=1, source_target_pairs={{0,4},{1,5},{2,6},{3,7},{4,0},{5,1},{6,2},{7,3},{8,12},{9,13},{10,... | collective-permute-start | bytes 1179656 | tf_op jit(solution)/shard_map/ppermute | solution.py:51
  23.4 9.9 %collective-permute-start.9 = (bf16[512,384]{1,0:T(8,128)(2,1)S(1)}, bf16[512,384]{1,0:T(8,128)(2,1)S(1)}, u32[]{:S(2)}, u32[]{:S(2)}) collective-permute-start(bf16[512,384]{1,0:T(8,128)(2,1)S(1)} %collective-permute-done.1.refs_2_), channel_id=1, source_target_pairs={{0,1},{1,0},{2,3},{3,2},{4,5},{5,4},{6,7},{7,6},{8,9},{9,8},{10,11... | collective-permute-start | bytes 1179656 | tf_op jit(solution)/shard_map/ppermute | solution.py:51
  23.4 13.4 %collective-permute-start.4 = (bf16[512,384]{1,0:T(8,128)(2,1)S(1)}, bf16[512,384]{1,0:T(8,128)(2,1)S(1)}, u32[]{:S(2)}, u32[]{:S(2)}) collective-permute-start(bf16[512,384]{1,0:T(8,128)(2,1)S(1)} %collective-permute-done.1.refs_2_), channel_id=1, source_target_pairs={{0,8},{1,9},{2,10},{3,11},{4,12},{5,13},{6,14},{7,15},{8,0},{9,1},... | collective-permute-start | bytes 1179656 | tf_op jit(solution)/shard_map/ppermute | solution.py:51
  25.6 15.8 %collective-permute-start.5 = (bf16[512,384]{1,0:T(8,128)(2,1)}, bf16[512,384]{1,0:T(8,128)(2,1)S(1)}, u32[]{:S(2)}, u32[]{:S(2)}) collective-permute-start(bf16[512,384]{1,0:T(8,128)(2,1)} %refs_0_.1), channel_id=1, source_target_pairs={{0,4},{1,5},{2,6},{3,7},{4,0},{5,1},{6,2},{7,3},{8,12},{9,13},{10,... | collective-permute-start | bytes 1179656 | tf_op jit(solution)/shard_map/ppermute | solution.py:51
  25.6 19.4 %collective-permute-start.3 = (bf16[512,384]{1,0:T(8,128)(2,1)S(1)}, bf16[512,384]{1,0:T(8,128)(2,1)}, u32[]{:S(2)}, u32[]{:S(2)}) collective-permute-start(bf16[512,384]{1,0:T(8,128)(2,1)S(1)} %collective-permute-done.refs_1_), channel_id=1, source_target_pairs={{0,8},{1,9},{2,10},{3,11},{4,12},{5,13},{6,14},{7,15},{8,0},{9,1},... | collective-permute-start | bytes 1179656 | tf_op jit(solution)/shard_map/ppermute | solution.py:51
  33.3 12.4 %collective-permute-start.8 = (bf16[512,384]{1,0:T(8,128)(2,1)S(1)}, bf16[512,384]{1,0:T(8,128)(2,1)}, u32[]{:S(2)}, u32[]{:S(2)}) collective-permute-start(bf16[512,384]{1,0:T(8,128)(2,1)S(1)} %collective-permute-done.refs_1_), channel_id=1, source_target_pairs={{0,1},{1,0},{2,3},{3,2},{4,5},{5,4},{6,7},{7,6},{8,9},{9,8},{10,11... | collective-permute-start | bytes 1179656 | tf_op jit(solution)/shard_map/ppermute | solution.py:51
  33.3 12.3 %collective-permute-start.14 = (bf16[512,384]{1,0:T(8,128)(2,1)S(1)}, bf16[512,384]{1,0:T(8,128)(2,1)}, u32[]{:S(2)}, u32[]{:S(2)}) collective-permute-start(bf16[512,384]{1,0:T(8,128)(2,1)S(1)} %collective-permute-done.6.refs_7_), channel_id=1, source_target_pairs={{0,1},{1,0},{2,3},{3,2},{4,5},{5,4},{6,7},{7,6},{8,9},{9,8},{10,11... | collective-permute-start | bytes 1179656 | tf_op jit(solution)/shard_map/ppermute | solution.py:51
  36.9 8.8 %collective-permute-start.12 = (bf16[512,384]{1,0:T(8,128)(2,1)S(1)}, bf16[512,384]{1,0:T(8,128)(2,1)}, u32[]{:S(2)}, u32[]{:S(2)}) collective-permute-start(bf16[512,384]{1,0:T(8,128)(2,1)S(1)} %collective-permute-done.4.refs_5_), channel_id=1, source_target_pairs={{0,1},{1,0},{2,3},{3,2},{4,5},{5,4},{6,7},{7,6},{8,9},{9,8},{10,11... | collective-permute-start | bytes 1179656 | tf_op jit(solution)/shard_map/ppermute | solution.py:51
  41.3 4.3 %collective-permute-start.13 = (bf16[512,384]{1,0:T(8,128)(2,1)S(1)}, bf16[512,384]{1,0:T(8,128)(2,1)}, u32[]{:S(2)}, u32[]{:S(2)}) collective-permute-start(bf16[512,384]{1,0:T(8,128)(2,1)S(1)} %collective-permute-done.5.refs_6_), channel_id=1, source_target_pairs={{0,1},{1,0},{2,3},{3,2},{4,5},{5,4},{6,7},{7,6},{8,9},{9,8},{10,11... | collective-permute-start | bytes 1179656 | tf_op jit(solution)/shard_map/ppermute | solution.py:51
  109.9 14.7 %collective-permute-start.15 = (bf16[8,512,384]{2,1,0:T(8,128)(2,1)S(1)}, bf16[8,512,384]{2,1,0:T(8,128)(2,1)S(1)}, u32[]{:S(2)}, u32[]{:S(2)}) collective-permute-start(bf16[8,512,384]{2,1,0:T(8,128)(2,1)S(1)} %get-tuple-element.25), channel_id=1, source_target_pairs={{0,1},{1,0},{2,3},{3,2},{4,5},{5,4},{6,7},{7,6},{8,9},{9,8},{10,11... | collective-permute-start | bytes 9437192 | tf_op jit(solution)/shard_map/ppermute | solution.py:51
  110.2 64.8 %collective-permute-start.25 = (bf16[8,384,256]{2,1,0:T(8,128)(2,1)}, bf16[8,384,256]{2,1,0:T(8,128)(2,1)S(1)}, u32[]{:S(2)}, u32[]{:S(2)}) collective-permute-start(bf16[8,384,256]{2,1,0:T(8,128)(2,1)} %weight_rows.4), channel_id=1, source_target_pairs={{0,128},{1,129},{2,130},{3,131},{4,132},{5,133},{6,134},{7,135},{8... | collective-permute-start | bytes 4718600 | tf_op jit(solution)/shard_map/ppermute | solution.py:51
  128.0 43.2 %collective-permute-start.16 = (bf16[2,512,384]{2,1,0:T(8,128)(2,1)}, bf16[2,512,384]{2,1,0:T(8,128)(2,1)}, u32[]{:S(2)}, u32[]{:S(2)}) collective-permute-start(bf16[2,512,384]{2,1,0:T(8,128)(2,1)} %get-tuple-element.37), channel_id=1, source_target_pairs={{0,2},{1,3},{2,4},{3,5},{4,6},{5,7},{6,0},{7,1},{8,10},{9,11},{10,... | collective-permute-start | bytes 2359304 | tf_op jit(solution)/shard_map/ppermute | solution.py:51
  128.0 43.2 %collective-permute-start.18 = (bf16[2,512,384]{2,1,0:T(8,128)(2,1)}, bf16[2,512,384]{2,1,0:T(8,128)(2,1)}, u32[]{:S(2)}, u32[]{:S(2)}) collective-permute-start(bf16[2,512,384]{2,1,0:T(8,128)(2,1)} %get-tuple-element.38), channel_id=1, source_target_pairs={{0,6},{1,7},{2,0},{3,1},{4,2},{5,3},{6,4},{7,5},{8,14},{9,15},{10,... | collective-permute-start | bytes 2359304 | tf_op jit(solution)/shard_map/ppermute | solution.py:51
  131.2 40.0 %collective-permute-start.17 = (bf16[2,512,384]{2,1,0:T(8,128)(2,1)}, bf16[2,512,384]{2,1,0:T(8,128)(2,1)}, u32[]{:S(2)}, u32[]{:S(2)}) collective-permute-start(bf16[2,512,384]{2,1,0:T(8,128)(2,1)} %get-tuple-element.39), channel_id=1, source_target_pairs={{0,4},{1,5},{2,6},{3,7},{4,0},{5,1},{6,2},{7,3},{8,12},{9,13},{10,... | collective-permute-start | bytes 2359304 | tf_op jit(solution)/shard_map/ppermute | solution.py:51
  132.8 24.9 %collective-permute-start.20 = (f32[8,128]{1,0:T(8,128)S(1)}, f32[8,128]{1,0:T(8,128)S(1)}, u32[]{:S(2)}, u32[]{:S(2)}) collective-permute-start(f32[8,128]{1,0:T(8,128)S(1)} %add.86), channel_id=1, source_target_pairs={{0,8},{1,9},{2,10},{3,11},{4,12},{5,13},{6,14},{7,15},{8,0},{9,1},... | collective-permute-start | bytes 12296 | tf_op jit(solution)/shard_map/ppermute | solution.py:51
  157.7 8.4 %collective-permute-start.21 = (f32[8,128]{1,0:T(8,128)S(1)}, f32[8,128]{1,0:T(8,128)S(1)}, u32[]{:S(2)}, u32[]{:S(2)}) collective-permute-start(f32[8,128]{1,0:T(8,128)S(1)} %add.87), channel_id=1, source_target_pairs={{0,2},{1,3},{2,4},{3,5},{4,6},{5,7},{6,0},{7,1},{8,10},{9,11},{10,... | collective-permute-start | bytes 12296 | tf_op jit(solution)/shard_map/ppermute | solution.py:51
  166.0 5.1 %collective-permute-start.22 = (f32[8,128]{1,0:T(8,128)S(1)}, f32[8,128]{1,0:T(8,128)S(1)}, u32[]{:S(2)}, u32[]{:S(2)}) collective-permute-start(f32[8,128]{1,0:T(8,128)S(1)} %add.88), channel_id=1, source_target_pairs={{0,4},{1,5},{2,6},{3,7},{4,0},{5,1},{6,2},{7,3},{8,12},{9,13},{10,... | collective-permute-start | bytes 12296 | tf_op jit(solution)/shard_map/ppermute | solution.py:51
  183.5 11.6 %collective-permute-start.26 = (bf16[384,256]{1,0:T(8,128)(2,1)S(1)}, bf16[384,256]{1,0:T(8,128)(2,1)S(1)}, u32[]{:S(2)}, u32[]{:S(2)}) collective-permute-start(bf16[384,256]{1,0:T(8,128)(2,1)S(1)} %get-tuple-element.44), channel_id=1, source_target_pairs={{0,16},{1,113},{2,18},{3,115},{4,20},{5,117},{6,22},{7,119},{8,24}... | collective-permute-start | bytes 589832 | tf_op jit(solution)/shard_map/ppermute | solution.py:51
  185.8 13.4 %collective-permute-start.30 = (bf16[384,256]{1,0:T(8,128)(2,1)S(1)}, bf16[384,256]{1,0:T(8,128)(2,1)S(1)}, u32[]{:S(2)}, u32[]{:S(2)}) collective-permute-start(bf16[384,256]{1,0:T(8,128)(2,1)S(1)} %get-tuple-element.45), channel_id=1, source_target_pairs={{0,112},{1,17},{2,114},{3,19},{4,116},{5,21},{6,118},{7,23},{8,120... | collective-permute-start | bytes 589832 | tf_op jit(solution)/shard_map/ppermute | solution.py:51
  195.2 7.0 %collective-permute-start.27 = (bf16[384,256]{1,0:T(8,128)(2,1)S(1)}, bf16[384,256]{1,0:T(8,128)(2,1)S(1)}, u32[]{:S(2)}, u32[]{:S(2)}) collective-permute-start(bf16[384,256]{1,0:T(8,128)(2,1)S(1)} %fusion.11), channel_id=1, source_target_pairs={{0,16},{1,113},{2,18},{3,115},{4,20},{5,117},{6,22},{7,119},{8,24}... | collective-permute-start | bytes 589832 | tf_op jit(solution)/shard_map/ppermute | solution.py:51
  195.6 20.1 %collective-permute-start.23 = (bf16[512,384]{1,0:T(8,128)(2,1)S(1)}, bf16[512,384]{1,0:T(8,128)(2,1)S(1)}, u32[]{:S(2)}, u32[]{:S(2)}) collective-permute-start(bf16[512,384]{1,0:T(8,128)(2,1)S(1)} %fusion.5), channel_id=1, source_target_pairs={{0,8},{1,9},{2,10},{3,11},{4,12},{5,13},{6,14},{7,15},{8,0},{9,1},... | collective-permute-start | bytes 1179656 | tf_op jit(solution)/shard_map/ppermute | solution.py:51
  202.3 7.0 %collective-permute-start.28 = (bf16[384,256]{1,0:T(8,128)(2,1)S(1)}, bf16[384,256]{1,0:T(8,128)(2,1)S(1)}, u32[]{:S(2)}, u32[]{:S(2)}) collective-permute-start(bf16[384,256]{1,0:T(8,128)(2,1)S(1)} %get-tuple-element.42), channel_id=1, source_target_pairs={{0,16},{1,113},{2,18},{3,115},{4,20},{5,117},{6,22},{7,119},{8,24}... | collective-permute-start | bytes 589832 | tf_op jit(solution)/shard_map/ppermute | solution.py:51
  202.4 7.8 %collective-permute-start.31 = (bf16[384,256]{1,0:T(8,128)(2,1)S(1)}, bf16[384,256]{1,0:T(8,128)(2,1)S(1)}, u32[]{:S(2)}, u32[]{:S(2)}) collective-permute-start(bf16[384,256]{1,0:T(8,128)(2,1)S(1)} %get-tuple-element.43), channel_id=1, source_target_pairs={{0,112},{1,17},{2,114},{3,19},{4,116},{5,21},{6,118},{7,23},{8,120... | collective-permute-start | bytes 589832 | tf_op jit(solution)/shard_map/ppermute | solution.py:51
  210.2 7.7 %collective-permute-start.29 = (bf16[384,256]{1,0:T(8,128)(2,1)S(1)}, bf16[384,256]{1,0:T(8,128)(2,1)}, u32[]{:S(2)}, u32[]{:S(2)}) collective-permute-start(bf16[384,256]{1,0:T(8,128)(2,1)S(1)} %get-tuple-element.40), channel_id=1, source_target_pairs={{0,16},{1,113},{2,18},{3,115},{4,20},{5,117},{6,22},{7,119},{8,24}... | collective-permute-start | bytes 589832 | tf_op jit(solution)/shard_map/ppermute | solution.py:51
  210.3 7.6 %collective-permute-start.32 = (bf16[384,256]{1,0:T(8,128)(2,1)S(1)}, bf16[384,256]{1,0:T(8,128)(2,1)}, u32[]{:S(2)}, u32[]{:S(2)}) collective-permute-start(bf16[384,256]{1,0:T(8,128)(2,1)S(1)} %get-tuple-element.41), channel_id=1, source_target_pairs={{0,112},{1,17},{2,114},{3,19},{4,116},{5,21},{6,118},{7,23},{8,120... | collective-permute-start | bytes 589832 | tf_op jit(solution)/shard_map/ppermute | solution.py:51
  215.1 7.9 %collective-permute-start.24 = (bf16[384,512]{1,0:T(8,128)(2,1)S(1)}, bf16[384,512]{1,0:T(8,128)(2,1)S(1)}, u32[]{:S(2)}, u32[]{:S(2)}) collective-permute-start(bf16[384,512]{1,0:T(8,128)(2,1)S(1)} %slice.101), channel_id=1, source_target_pairs={{0,128},{1,129},{2,130},{3,131},{4,132},{5,133},{6,134},{7,135},{8... | collective-permute-start | bytes 1179656 | tf_op jit(solution)/shard_map/ppermute | solution.py:51
  (25 other events, 232.2 us)
Sparse Core Ops, SparseCore 0:
  91.5 82.9 reduce-scatter.1
